TPU v7x, 32 devices: a whole 2x2x4 slice. The times are simulated.
32 devices in a mesh: neur: 16 (over z, y, core), tm: 2 (over x).
Axes of the slice: x: 2, y: 2, z: 4, core: 2. Of those that a mesh axis runs over, the one named last changes fastest.
Arguments:
- spikes: int32 [512, 32768], P(None, ('neur', 'tm')), may hold values from 0 to 9
- held_in: int32 [32768], P(('neur', 'tm')), may hold values 0 or 1
- readin_weight: bfloat16 [32768, 1024], P(('neur', 'tm')), may hold values from -0.03125 to 0.03125
- qkv_weight: bfloat16 [1024, 3, 1024], P(None, None, 'tm'), may hold values from -0.1875 to 0.1875
- out_weight: bfloat16 [1024, 1024], P('tm'), may hold values from -0.1875 to 0.1875
- up_weight: bfloat16 [1024, 4096], P(None, 'tm'), may hold values from -0.1875 to 0.1875
- down_weight: bfloat16 [4096, 1024], P('tm'), may hold values from -0.09375 to 0.09375
- norm_gain: float32 [1024], replicated, may hold values from 0.25 to 1.75
- mlp_gain: float32 [1024], replicated, may hold values from 0.25 to 1.75
- final_gain: float32 [1024], replicated, may hold values from 0.25 to 1.75
- readout_weight: bfloat16 [32768, 1024], P(('neur', 'tm')), may hold values from -0.1875 to 0.1875
- readout_bias: float32 [32768], P(('neur', 'tm')), may hold values from -3 to 3
Outputs:
- latents: bfloat16 [512, 1024], P('neur')
- neuron_bits: float32 [32768], P(('neur', 'tm'))
- bits_per_spike: float32 [], replicated
All inputs are finite; a program needn't handle non-finite values. No bound on the sum of `held_in` on one device may be relied on, other than what follows from the above.
Results may differ from a plain program's by a relative error of at most 0.006.
Values may be sent and summed in bfloat16 or wider, within the bound.
A program may use at most 64 MiB of HBM per device.

v0:
```python
import math

import jax
import jax.numpy as jnp
from jax import lax
from jax.sharding import PartitionSpec as P

HEAD_DIM = 128


def normed(values, gain_vec):
    return values * lax.rsqrt(jnp.mean(values * values, -1, keepdims=True) + 1e-05) * gain_vec


def on_device(
    spikes,
    held_in,
    readin_weight,
    qkv_weight,
    out_weight,
    up_weight,
    down_weight,
    norm_gain,
    mlp_gain,
    final_gain,
    readout_weight,
    readout_bias,
):
    frames_all = spikes.shape[0]
    rows_here = frames_all // lax.axis_size("neur")
    masked = (spikes * held_in[None, :]).astype(jnp.bfloat16)
    heldout = (1 - held_in).astype(jnp.float32)
    counts = jnp.sum(spikes, 0).astype(jnp.float32)
    partial_sum = jnp.dot(masked, readin_weight, preferred_element_type=jnp.float32)
    summed = lax.psum(partial_sum, ("neur", "tm"))
    stream = lax.dynamic_slice_in_dim(summed, lax.axis_index("neur") * rows_here, rows_here, 0)
    model_dim = stream.shape[1]
    head_cols = qkv_weight.shape[2]
    local_heads = head_cols // HEAD_DIM
    attn_in = normed(stream, norm_gain).astype(jnp.bfloat16)
    projected = jnp.dot(
        attn_in, qkv_weight.reshape(model_dim, 3 * head_cols), preferred_element_type=jnp.float32
    ).astype(jnp.bfloat16)
    queries = projected[:, :head_cols].reshape(rows_here, local_heads, HEAD_DIM)
    keys_local = projected[:, head_cols : 2 * head_cols]
    values_local = projected[:, 2 * head_cols :]
    scaling = 1.0 / math.sqrt(HEAD_DIM)
    key_rows = lax.all_gather(keys_local, "neur", axis=0, tiled=True).reshape(
        -1, local_heads, HEAD_DIM
    )
    value_rows = lax.all_gather(values_local, "neur", axis=0, tiled=True).reshape(
        -1, local_heads, HEAD_DIM
    )
    scores = (
        jnp.einsum("qhd,khd->hqk", queries, key_rows, preferred_element_type=jnp.float32) * scaling
    )
    weights = jnp.exp(scores)
    numerator = jnp.einsum(
        "hqk,khd->qhd", weights.astype(jnp.bfloat16), value_rows, preferred_element_type=jnp.float32
    )
    denominator = jnp.sum(weights, -1).T
    numerator, denominator = (numerator, denominator)
    heads_out = (
        (numerator / denominator[:, :, None]).astype(jnp.bfloat16).reshape(rows_here, head_cols)
    )
    attn_part = jnp.dot(heads_out, out_weight, preferred_element_type=jnp.float32)
    mixed_state = stream + lax.psum(attn_part, "tm")
    mlp_in = normed(mixed_state, mlp_gain).astype(jnp.bfloat16)
    hidden_act = jax.nn.gelu(jnp.dot(mlp_in, up_weight, preferred_element_type=jnp.float32)).astype(
        jnp.bfloat16
    )
    mlp_part = jnp.dot(hidden_act, down_weight, preferred_element_type=jnp.float32)
    final_state = mixed_state + lax.psum(mlp_part, "tm")
    latents = normed(final_state, final_gain).astype(jnp.bfloat16)
    log_rate = (
        lax.dot_general(
            lax.all_gather(latents, "neur", axis=0, tiled=True),
            readout_weight,
            (((1,), (1,)), ((), ())),
            preferred_element_type=jnp.float32,
        )
        + readout_bias[None, :]
    )
    observed = spikes.astype(jnp.float32)
    model_ll = jnp.sum(observed * log_rate - jnp.exp(log_rate), 0)
    null_ll = counts * jnp.log((counts + 1.0) / frames_all) - (counts + 1.0)
    gained = heldout * (model_ll - null_ll)
    neuron_bits = gained / (math.log(2.0) * (counts + 1.0))
    score_sum, spike_sum = lax.psum((jnp.sum(gained), jnp.sum(heldout * counts)), ("neur", "tm"))
    bits_total = score_sum / (math.log(2.0) * (1.0 + spike_sum))
    return (latents, neuron_bits, bits_total)


def solution(mesh):
    in_specs = (
        P(None, ("neur", "tm")),
        P(("neur", "tm")),
        P(("neur", "tm"), None),
        P(None, None, "tm"),
        P("tm", None),
        P(None, "tm"),
        P("tm", None),
        P(),
        P(),
        P(),
        P(("neur", "tm"), None),
        P(("neur", "tm")),
    )
    out_specs = (P("neur", None), P(("neur", "tm")), P())
    return jax.shard_map(
        on_device, mesh=mesh, in_specs=in_specs, out_specs=out_specs, check_vma=False
    )
```

profile of v0, /device:TPU:0, one launch (start us, length us, event | category | flops | bytes accessed | tf_op | source)
XLA Modules:
  0.0 338.0 jit_solution(17783210301829643834)
XLA Ops:
  7.2 1.5 copy-done
  8.8 4.2 %fusion.4 = f32[512,1024]{1,0:T(8,128)} fusion(bf16[1024,1024]{1,0:T(8,128)(2,1)S(1)} %copy-done, s32[512,1024]{1,0:T(8,128)} %param.12, s32[1024]{0:T(1024)} %param.13), kind=kOutput, calls=%fused_computation.9 | convolution fusion | flops 1074790400 | bytes 6295552 | tf_op jit(solution)/shard_map/dot_general | solution.py:34
  13.0 0.0 all-reduce.7.cloned.1.call-start
  13.1 4.7 %copy.18 = bf16[1024,3,512]{0,2,1:T(8,128)(2,1)} copy(bf16[1024,3,512]{2,0,1:T(8,128)(2,1)} %param.15) | data formatting | bytes 6291456 | tf_op args[3]
  17.8 132.1 %all-reduce.5.cloned.1.call-done = f32[512,1024]{1,0:T(8,128)} async-done(((f32[512,1024]{1,0:T(8,128)}), f32[512,1024]{1,0:T(8,128)}) %all-reduce.5.cloned.1.call-update) | async-done | bytes 2097168 | tf_op jit(solution)/shard_map/psum | solution.py:35
  149.9 1.0 multiply_reduce_fusion.2
  150.9 3.0 convolution_convert_fusion
  154.0 21.7 %all_gather.10 = bf16[512,512]{1,0:T(8,128)(2,1)S(1)} all-gather(bf16[32,512]{1,0:T(8,128)(2,1)S(1)} %get-tuple-element.12), channel_id=1, replica_groups=mesh['neur'=16,'tm'=2] {'neur'}, dimensions={0}, use_global_device_ids=true | all-gather | bytes 557056 | tf_op jit(solution)/shard_map/all_gather | solution.py:48
  175.7 19.0 %all_gather.9 = bf16[512,512]{1,0:T(8,128)(2,1)S(1)} all-gather(bf16[32,512]{1,0:T(8,128)(2,1)S(1)} %get-tuple-element.13), channel_id=1, replica_groups=mesh['neur'=16,'tm'=2] {'neur'}, dimensions={0}, use_global_device_ids=true | all-gather | bytes 557056 | tf_op jit(solution)/shard_map/all_gather | solution.py:51
  194.7 0.4 fusion.43
  195.0 0.2 fusion.3
  195.3 0.9 fusion.32
  196.2 0.0 all-reduce.9.cloned.1.call-start
  196.3 19.1 %all-reduce.7.cloned.1.call-done = f32[32,1024]{1,0:T(8,128)} async-done(((f32[32,1024]{1,0:T(8,128)}), f32[32,1024]{1,0:T(8,128)}) %all-reduce.7.cloned.1.call-update) | async-done | bytes 131088 | tf_op jit(solution)/shard_map/psum | solution.py:67
  215.4 1.1 multiply_reduce_fusion.1
  216.5 5.7 %fusion.18 = f32[32,1024]{1,0:T(8,128)} fusion(bf16[2048,1024]{1,0:T(8,128)(2,1)} %param.18, bf16[1024,2048]{1,0:T(8,128)(2,1)} %param.17, f32[32,1024]{1,0:T(8,128)S(1)} %get-tuple-element.10, f32[1024]{0:T(1024)S(1)} %copy-done.3, f32[32]{0:T(128)S(1)} %add_rsqrt_fusion.1), kind=kOutput, calls=%fused_computation.24 | convolution fusion | flops 269123584 | bytes 8654976 | tf_op jit(solution)/shard_map/dot_general | solution.py:72
  222.3 21.5 %all-reduce.9.cloned.1.call-done = f32[32,1024]{1,0:T(8,128)} async-done(((f32[32,1024]{1,0:T(8,128)}), f32[32,1024]{1,0:T(8,128)}) %all-reduce.9.cloned.1.call-update) | async-done | bytes 131088 | tf_op jit(solution)/shard_map/psum | solution.py:73
  243.9 1.0 multiply_reduce_fusion
  244.9 0.7 multiply_convert_fusion.2
  245.7 1.7 reduce_sum.77
  247.4 37.3 %all-gather.2.cloned.1.call-done = bf16[512,1024]{1,0:T(8,128)(2,1)} async-done(((bf16[32,1024]{1,0:T(8,128)(2,1)}), bf16[512,1024]{1,0:T(8,128)(2,1)}) %all-gather.2.cloned.1.call-update) | async-done | bytes 1048592 | tf_op jit(solution)/shard_map/all_gather | solution.py:77
  284.7 4.1 %subtract_reduce_fusion = f32[1024]{0:T(1024)S(1)} fusion(s32[512,1024]{1,0:T(8,128)} %param.12, bf16[512,1024]{1,0:T(8,128)(2,1)} %all-gather.2.cloned.1.call-done, bf16[1024,1024]{1,0:T(8,128)(2,1)} %param.22, f32[1024]{0:T(1024)S(1)} %copy-done.6), kind=kOutput, calls=%fused_computation.1 | convolution fusion | flops 1076362240 | bytes 5251072 | tf_op jit(solution)/shard_map/dot_general | solution.py:76
  288.8 1.3 multiply_reduce_fusion.3
  290.0 39.1 %all-reduce = (f32[]{:T(128)}, f32[]{:T(128)}) all-reduce(f32[]{:T(128)} %get-tuple-element.4, f32[]{:T(128)} %get-tuple-element.3), channel_id=1, replica_groups=mesh['neur'=16,'tm'=2] {'neur','tm'}, use_global_device_ids=true, to_apply=%region_10.0 | all-reduce | flops 2 | bytes 16 | tf_op jit(solution)/shard_map/psum | solution.py:89
  (23 shorter events, 0.2 us)
Async XLA Ops:
  7.2 1.6 copy-start
  7.2 142.7 %all-reduce.5.cloned.1.call-start = ((), (), s32[]{:S(2)}) async-start(), calls=%async_computation | async-start | bytes 4194304 | tf_op jit(solution)/shard_map/psum | solution.py:35
  13.0 202.4 %all-reduce.7.cloned.1.call-start = ((), (), s32[]{:S(2)}) async-start(), calls=%async_computation.1 | async-start | bytes 262144 | tf_op jit(solution)/shard_map/psum | solution.py:67
  13.1 137.9 %copy-start.2 = (f32[1024]{0:T(1024)S(1)}, f32[1024]{0:T(1024)}, u32[]{:S(2)}) copy-start(f32[1024]{0:T(1024)} %param.19) | copy-start | bytes 12292
  154.0 41.3 %copy-start.1 = (bf16[512,1024]{1,0:T(8,128)(2,1)S(1)}, bf16[512,1024]{1,0:T(8,128)(2,1)}, u32[]{:S(2)}) copy-start(bf16[512,1024]{1,0:T(8,128)(2,1)} %param.16) | copy-start | bytes 3145732
  175.7 40.8 %copy-start.3 = (f32[1024]{0:T(1024)S(1)}, f32[1024]{0:T(1024)}, u32[]{:S(2)}) copy-start(f32[1024]{0:T(1024)} %param.20) | copy-start | bytes 12292
  196.2 47.7 %all-reduce.9.cloned.1.call-start = ((), (), s32[]{:S(2)}) async-start(), calls=%async_computation.2 | async-start | bytes 262144 | tf_op jit(solution)/shard_map/psum | solution.py:73
  216.5 28.4 %copy-start.4 = (f32[1024]{0:T(1024)S(1)}, f32[1024]{0:T(1024)}, u32[]{:S(2)}) copy-start(f32[1024]{0:T(1024)} %param.21) | copy-start | bytes 12292
  222.3 62.4 %copy-start.6 = (f32[1024]{0:T(1024)S(1)}, f32[1024]{0:T(1024)}, u32[]{:S(2)}) copy-start(f32[1024]{0:T(1024)} %param.23) | copy-start | bytes 12292
  222.3 62.4 %all-gather.2.cloned.1.call-start = ((), (), s32[]{:S(2)}) async-start(), calls=%async_computation.3 | async-start | bytes 1114112 | tf_op jit(solution)/shard_map/all_gather | solution.py:77
  247.4 41.3 %copy-start.5 = (s32[1024]{0:T(1024)S(1)}, s32[1024]{0:T(1024)}, u32[]{:S(2)}) copy-start(s32[1024]{0:T(1024)} %param.13) | copy-start | bytes 12292
Sparse Core Ops, SparseCore 0:
  13.3 136.4 all-reduce.4
  196.3 19.0 all-reduce.6
  222.4 21.4 all-reduce.8
  246.7 37.9 all-gather.1
where the time goes:
time: 339 us; the launch traced here: 338 us
  waiting for transfers between devices  210 us (62%)
  blocking collectives  79.8 us (24%)
  matrix products  18.5 us (5%)
  between operations  16.2 us (5%)
  other arithmetic  6.91 us (2%)
  local copies, waits for them, and re-layouts  6.27 us (2%)
    psum x1, waiting for transfers between devices, on_device(): summed = lax.psum(partial_sum, ('neur', 'tm'))  132 us
    psum x1, blocking collectives, on_device(): lax.psum((jnp.sum(gained), jnp.sum(heldout * counts)), ('neur', 'tm'))  39.1 us
    all_gather x1, waiting for transfers between devices, on_device(): lax.all_gather(latents, 'neur', axis=0, tiled=True)  37.3 us
    all_gather x1, blocking collectives, on_device(): lax.all_gather(keys_local, 'neur', axis=0, tiled=True)  21.7 us
    psum x1, waiting for transfers between devices, on_device(): final_state = mixed_state + lax.psum(mlp_part, 'tm')  21.5 us
    psum x1, waiting for transfers between devices, on_device(): mixed_state = stream + lax.psum(attn_part, 'tm')  19.1 us
    all_gather x1, blocking collectives, on_device(): lax.all_gather(values_local, 'neur', axis=0, tiled=True)  19 us
  transfers between devices with their start and end apart: 4, of which 4 were waited for; matrix products, arithmetic and copies ran while one was open for 2% of the time, Pallas kernels for 0%

commit v1 on v0

v1 whole, which is shorter than its diff:
```python
import functools
import math

import jax
import jax.numpy as jnp
from jax import lax
from jax.experimental import pallas as pl
from jax.experimental.pallas import tpu as pltpu
from jax.sharding import PartitionSpec as P

HEAD_DIM = 128
OUTER = 4
MESH = pl.DeviceIdType.MESH
BF = jnp.bfloat16
F32 = jnp.float32


def normed(values, gain_vec):
    return values * lax.rsqrt(jnp.mean(values * values, -1, keepdims=True) + 1e-05) * gain_vec


def dot(a, b):
    return jnp.dot(a, b, preferred_element_type=F32)


def dot_nt(a, b):
    return lax.dot_general(a, b, (((1,), (1,)), ((), ())), preferred_element_type=F32)


def kernel(
    n_size,
    t_size,
    spikes_h,
    held_ref,
    readin_h,
    qkv_h,
    out_h,
    up_h,
    down_h,
    ng_ref,
    mg_ref,
    fg_ref,
    readout_h,
    bias_ref,
    lat_out,
    bits_out,
    tot_out,
    spikes_v,
    readin_v,
    qkv_v,
    out_v,
    up_v,
    down_v,
    readout_v,
    load_sems,
    pp,
    core_s,
    core_r,
    s1,
    mid_s,
    mid_r,
    out_s,
    out_r,
    tsum,
    kv,
    lat,
    hid,
    fin,
    core_sems,
    mid_sems,
    outer_sems,
    t_sems,
    kv_sems,
    lat_sems,
    fin_sems,
):
    mid_size = n_size // (2 * OUTER)
    frames, neurons = spikes_v.shape
    rows = frames // n_size
    width = readin_v.shape[1]
    head_cols = out_v.shape[0]
    group = 2 * mid_size * rows
    n = lax.axis_index("neur")
    t = lax.axis_index("tm")
    c = lax.rem(n, 2)
    m = lax.rem(lax.div(n, 2), mid_size)
    o = lax.div(n, 2 * mid_size)

    def nid(oo, mm, cc):
        return (oo * mid_size + mm) * 2 + cc

    def rot(v, d, size):
        return lax.rem(v + d, size)

    def core_peer():
        return (nid(o, m, 1 - c), t)

    def mid_peer(d):
        return (nid(o, rot(m, d, mid_size), c), t)

    def outer_peer(d):
        return (nid(rot(o, d, OUTER), m, c), t)

    def t_peer(d):
        return (n, rot(t, d, t_size))

    loads = []
    for i, (src, dst) in enumerate(
        (
            (spikes_h, spikes_v),
            (readin_h, readin_v),
            (qkv_h, qkv_v),
            (out_h, out_v),
            (up_h, up_v),
            (down_h, down_v),
            (readout_h, readout_v),
        )
    ):
        cp = pltpu.make_async_copy(src, dst, load_sems.at[i])
        cp.start()
        loads.append(cp)

    peers = [core_peer()]
    peers += [mid_peer(d) for d in range(1, mid_size)]
    peers += [outer_peer(d) for d in range(1, OUTER)]
    peers += [t_peer(d) for d in range(1, t_size)]
    barrier = pltpu.get_barrier_semaphore()
    for peer in peers:
        pl.semaphore_signal(barrier, inc=1, device_id=peer, device_id_type=MESH)

    sent = []

    def send(src, dst, sems, index, peer):
        cp = pltpu.make_async_remote_copy(
            src_ref=src,
            dst_ref=dst,
            send_sem=sems.at[(0,) + index],
            recv_sem=sems.at[(1,) + index],
            device_id=peer,
            device_id_type=MESH,
        )
        cp.start()
        sent.append(cp)
        return cp

    def sum_over_t(which, value):
        tsum[which, t] = value.astype(BF)
        cps = [
            send(tsum.at[which, t], tsum.at[which, t], t_sems, (which, d), t_peer(d))
            for d in range(1, t_size)
        ]
        for cp in cps:
            cp.wait_recv()
        total = tsum[which, 0].astype(F32)
        for i in range(1, t_size):
            total = total + tsum[which, i].astype(F32)
        return total

    def gather(buf, sems):
        cps = {}

        def push(do, dm, dc):
            if dc:
                own_m = rot(m, mid_size - dm, mid_size)
                own_o = rot(o, OUTER - do, OUTER)
                peer = core_peer()
            elif dm:
                own_m, own_o = m, rot(o, OUTER - do, OUTER)
                peer = mid_peer(dm)
            else:
                own_m, own_o = m, o
                peer = outer_peer(do)
            block = nid(own_o, own_m, c)
            cps[do, dm, dc] = send(
                buf.at[block], buf.at[block], sems, ((do * mid_size + dm) * 2 + dc,), peer
            )

        for d in range(1, OUTER):
            push(d, 0, 0)
        for d in range(1, mid_size):
            push(0, d, 0)
        push(0, 0, 1)
        for d in range(1, mid_size):
            cps[0, d, 0].wait_recv()
            push(0, d, 1)
        for do in (1, 3, 2):
            cps[do, 0, 0].wait_recv()
            for d in range(1, mid_size):
                push(do, d, 0)
            push(do, 0, 1)
        for do in (1, 3, 2):
            for d in range(1, mid_size):
                cps[do, d, 0].wait_recv()
                push(do, d, 1)
        for do in range(OUTER):
            for d in range(mid_size):
                cps[do, d, 1].wait_recv()

    loads[0].wait()
    loads[1].wait()
    held = held_ref[...]
    order = [2, 1, 3, 0]
    core_cps = {}
    for k, d in enumerate(order):
        at = pl.multiple_of(rot(o, d, OUTER) * group, group)
        masked = (spikes_v[pl.ds(at, group), :] * held).astype(F32).astype(BF)
        pp[d] = dot(masked, readin_v[...]).reshape(mid_size, 2, rows, width)
        for i in range(mid_size):
            core_s[d, i] = pp[d, i, 1 - c].astype(BF)
        if k == 0:
            pl.semaphore_wait(barrier, len(peers))
        core_cps[d] = send(core_s.at[d], core_r.at[d], core_sems, (d,), core_peer())
    mid_cps = {}
    for d in order:
        core_cps[d].wait_recv()
        for dm in list(range(1, mid_size)) + [0]:
            mm = rot(m, dm, mid_size)
            value = pp[d, mm, c] + core_r[d, mm].astype(F32)
            if dm:
                mid_s[d, dm] = value.astype(BF)
                mid_cps[d, dm] = send(
                    mid_s.at[d, dm], mid_r.at[d, dm], mid_sems, (d * mid_size + dm,), mid_peer(dm)
                )
            else:
                s1[d] = value
    outer_cps = {}
    for d in order:
        value = s1[d]
        for dm in range(1, mid_size):
            mid_cps[d, dm].wait_recv()
            value = value + mid_r[d, dm].astype(F32)
        if d:
            out_s[d] = value.astype(BF)
            outer_cps[d] = send(out_s.at[d], out_r.at[d], outer_sems, (d,), outer_peer(d))
    for d in (1, 3, 2):
        outer_cps[d].wait_recv()
        value = value + out_r[d].astype(F32)
    stream = sum_over_t(0, value)

    attn_in = normed(stream, ng_ref[...]).astype(BF)
    loads[2].wait()
    kv[n, :, :head_cols] = dot(attn_in, qkv_v[1]).astype(BF)
    kv[n, :, head_cols:] = dot(attn_in, qkv_v[2]).astype(BF)
    queries = dot(attn_in, qkv_v[0]).astype(BF)
    gather(kv, kv_sems)

    scaling = 1.0 / math.sqrt(HEAD_DIM)
    loads[3].wait()
    heads = []
    for h in range(head_cols // HEAD_DIM):
        cols = slice(h * HEAD_DIM, (h + 1) * HEAD_DIM)
        vcols = slice(head_cols + h * HEAD_DIM, head_cols + (h + 1) * HEAD_DIM)
        keys = kv[:, :, cols].reshape(frames, HEAD_DIM)
        values = kv[:, :, vcols].reshape(frames, HEAD_DIM)
        weights = jnp.exp(dot_nt(queries[:, cols], keys) * scaling)
        denominator = jnp.sum(weights, -1, keepdims=True)
        heads.append((dot(weights.astype(BF), values) / denominator).astype(BF))
    heads_out = heads[0] if len(heads) == 1 else jnp.concatenate(heads, -1)
    mixed_state = stream + sum_over_t(1, dot(heads_out, out_v[...]))

    mlp_in = normed(mixed_state, mg_ref[...]).astype(BF)
    loads[4].wait()
    tile = min(512, up_v.shape[1])
    for i in range(up_v.shape[1] // tile):
        cols = slice(i * tile, (i + 1) * tile)
        hid[:, cols] = jax.nn.gelu(dot(mlp_in, up_v[:, cols])).astype(BF)
    loads[5].wait()
    final_state = mixed_state + sum_over_t(2, dot(hid[...], down_v[...]))
    latents = normed(final_state, fg_ref[...]).astype(BF)
    lat_out[...] = latents
    lat[n] = latents
    gather(lat, lat_sems)

    loads[6].wait()
    blocks = 128 // rows

    def readout_step(i, carry):
        ll, counts = carry
        at = pl.multiple_of(i * blocks * rows, blocks * rows)
        piece = lat[pl.ds(i * blocks, blocks)].reshape(blocks * rows, width)
        log_rate = dot_nt(piece, readout_v[...]) + bias_ref[...]
        observed = spikes_v[pl.ds(at, blocks * rows), :].astype(F32)
        ll = ll + jnp.sum(observed * log_rate - jnp.exp(log_rate), 0, keepdims=True)
        return ll, counts + jnp.sum(observed, 0, keepdims=True)

    zero = jnp.zeros((1, neurons), F32)
    model_ll, counts = lax.fori_loop(0, n_size // blocks, readout_step, (zero, zero))
    heldout = (1 - held).astype(F32)
    null_ll = counts * jnp.log((counts + 1.0) / frames) - (counts + 1.0)
    gained = heldout * (model_ll - null_ll)
    bits_out[...] = gained / (math.log(2.0) * (counts + 1.0))
    score = jnp.sum(gained, -1, keepdims=True)
    spike_sum = jnp.sum(heldout * counts, -1, keepdims=True)
    lane = lax.broadcasted_iota(jnp.int32, (8, 128), 1)
    total = jnp.where(lane == 0, score, jnp.where(lane == 1, spike_sum, 0.0))

    base = 0
    for size, here, peer_of in (
        (2, c, lambda d: core_peer()),
        (mid_size, m, mid_peer),
        (t_size, t, t_peer),
        (OUTER, o, outer_peer),
    ):
        fin[base + here] = total
        cps = [
            send(fin.at[base + here], fin.at[base + here], fin_sems, (base + d,), peer_of(d))
            for d in range(1, size)
        ]
        for cp in cps:
            cp.wait_recv()
        total = fin[base]
        for i in range(1, size):
            total = total + fin[base + i]
        base += size
    score = jnp.sum(jnp.where(lane == 0, total, 0.0), -1, keepdims=True)
    spike_sum = jnp.sum(jnp.where(lane == 1, total, 0.0), -1, keepdims=True)
    tot_out[...] = jnp.broadcast_to(score / (math.log(2.0) * (1.0 + spike_sum)), (8, 128))
    for cp in sent:
        cp.wait_send()


def on_device(
    n_size,
    t_size,
    spikes,
    held_in,
    readin_weight,
    qkv_weight,
    out_weight,
    up_weight,
    down_weight,
    norm_gain,
    mlp_gain,
    final_gain,
    readout_weight,
    readout_bias,
):
    frames, neurons = spikes.shape
    width = readin_weight.shape[1]
    rows = frames // n_size
    mid = n_size // (2 * OUTER)
    head_cols = qkv_weight.shape[2]
    qkv = qkv_weight.transpose(1, 0, 2)
    row = lambda v: v.reshape(1, -1)
    vmem = pl.BlockSpec(memory_space=pltpu.VMEM)
    hbm = pl.BlockSpec(memory_space=pl.ANY)
    dma = pltpu.SemaphoreType.DMA
    n_fin = 2 + mid + t_size + OUTER
    latents, bits, total = pl.pallas_call(
        functools.partial(kernel, n_size, t_size),
        out_shape=(
            jax.ShapeDtypeStruct((rows, width), BF),
            jax.ShapeDtypeStruct((1, neurons), F32),
            jax.ShapeDtypeStruct((8, 128), F32),
        ),
        in_specs=[hbm, vmem, hbm, hbm, hbm, hbm, hbm, vmem, vmem, vmem, hbm, vmem],
        out_specs=(vmem, vmem, vmem),
        scratch_shapes=[
            pltpu.VMEM(spikes.shape, jnp.int32),
            pltpu.VMEM(readin_weight.shape, BF),
            pltpu.VMEM(qkv.shape, BF),
            pltpu.VMEM(out_weight.shape, BF),
            pltpu.VMEM(up_weight.shape, BF),
            pltpu.VMEM(down_weight.shape, BF),
            pltpu.VMEM(readout_weight.shape, BF),
            dma((7,)),
            pltpu.VMEM((OUTER, mid, 2, rows, width), F32),
            pltpu.VMEM((OUTER, mid, rows, width), BF),
            pltpu.VMEM((OUTER, mid, rows, width), BF),
            pltpu.VMEM((OUTER, rows, width), F32),
            pltpu.VMEM((OUTER, mid, rows, width), BF),
            pltpu.VMEM((OUTER, mid, rows, width), BF),
            pltpu.VMEM((OUTER, rows, width), BF),
            pltpu.VMEM((OUTER, rows, width), BF),
            pltpu.VMEM((3, t_size, rows, width), BF),
            pltpu.VMEM((n_size, rows, 2 * head_cols), BF),
            pltpu.VMEM((n_size, rows, width), BF),
            pltpu.VMEM((rows, up_weight.shape[1]), BF),
            pltpu.VMEM((n_fin, 8, 128), F32),
            dma((2, OUTER)),
            dma((2, OUTER * mid)),
            dma((2, OUTER)),
            dma((2, 3, t_size)),
            dma((2, n_size)),
            dma((2, n_size)),
            dma((2, n_fin)),
        ],
        compiler_params=pltpu.CompilerParams(
            collective_id=0, has_side_effects=True, vmem_limit_bytes=52 * 1024 * 1024
        ),
        cost_estimate=pl.CostEstimate(
            flops=4 * frames * neurons * width,
            bytes_accessed=20 * 1024 * 1024,
            transcendentals=frames * neurons,
        ),
    )(
        spikes,
        row(held_in),
        readin_weight,
        qkv,
        out_weight,
        up_weight,
        down_weight,
        row(norm_gain),
        row(mlp_gain),
        row(final_gain),
        readout_weight,
        row(readout_bias),
    )
    return latents, bits.reshape(neurons), total[0, 0]


def solution(mesh):
    in_specs = (
        P(None, ("neur", "tm")),
        P(("neur", "tm")),
        P(("neur", "tm"), None),
        P(None, None, "tm"),
        P("tm", None),
        P(None, "tm"),
        P("tm", None),
        P(),
        P(),
        P(),
        P(("neur", "tm"), None),
        P(("neur", "tm")),
    )
    out_specs = (P("neur", None), P(("neur", "tm")), P())
    return jax.shard_map(
        functools.partial(on_device, mesh.shape["neur"], mesh.shape["tm"]),
        mesh=mesh,
        in_specs=in_specs,
        out_specs=out_specs,
        check_vma=False,
    )
```

time: 339 us -> 74.7 us (0.22)
  waiting for transfers between devices: 210 us -> 0 us
  blocking collectives: 79.8 us -> 0 us
  Pallas kernels: 0 us -> 67.4 us
  matrix products: 18.5 us -> 0 us
  between operations: 16.2 us -> 0.66 us
  other arithmetic: 6.91 us -> 0 us
    psum x3 -> x0, waiting for transfers between devices: 173 us -> none  [the longest x1 132 us: on_device(): summed = lax.psum(partial_sum, ('neur', 'tm'))]
    pallas_call x0 -> x1, Pallas kernels: none -> 67.4 us  [on_device(): pl.pallas_call(functools.partial(kernel, n_size, t_size), out_shape=(jax....]
    all_gather x2 -> x0, blocking collectives: 40.7 us -> none  [the longest x1 21.7 us: on_device(): lax.all_gather(keys_local, 'neur', axis=0, tiled=True)]
    psum x1 -> x0, blocking collectives: 39.1 us -> none  [on_device(): lax.psum((jnp.sum(gained), jnp.sum(heldout * counts)), ('neur', 'tm'))]
    all_gather x1 -> x0, waiting for transfers between devices: 37.3 us -> none  [on_device(): lax.all_gather(latents, 'neur', axis=0, tiled=True)]
    dot_general x7 -> x0, matrix products: 18.5 us -> none  [the longest x1 5.74 us: on_device(): jnp.dot(hidden_act, down_weight, preferred_element_type=jnp.float32)]
    reduce_sum x5 -> x0, other arithmetic: 6.17 us -> none  [the longest x3 3.14 us: normed(): jnp.mean(values * values, -1, keepdims=True) + 1e-05]
  transfers between devices with their start and end apart: 4 -> 0, of which waited for: 4 -> 0; matrix products, arithmetic and copies ran while one was open for 2% -> 0% of each run, Pallas kernels for 0% -> 0%
where the time goes in v1:
time: 74.7 us; the launch traced here: 74.4 us
  Pallas kernels  67.4 us (90%)
  local copies, waits for them, and re-layouts  6.38 us (9%)
    pallas_call x1, Pallas kernels, on_device(): pl.pallas_call(functools.partial(kernel, n_size, t_size), out_shape=(jax....  67.4 us
    unnamed x14, local copies, waits for them, and re-layouts  5.87 us

profile of v1, /device:TPU:0, one launch (start us, length us, event | category | flops | bytes accessed | tf_op | source)
XLA Modules:
  0.0 74.4 jit_solution(1960067171347950340)
XLA Ops:
  0.6 0.0 copy-start
  0.6 1.2 %copy-done = bf16[512,1024]{1,0:T(8,128)(2,1)S(1)} copy-done((bf16[512,1024]{1,0:T(8,128)(2,1)S(1)}, bf16[512,1024]{1,0:T(8,128)(2,1)}, u32[]{:S(2)}) %copy-start) | copy-done | bytes 1048600
  1.9 0.0 copy-start.1
  1.9 0.7 copy-done.1
  2.5 0.0 copy-start.2
  2.6 0.7 copy-done.2
  3.2 0.0 copy-start.3
  3.2 0.7 copy-done.3
  3.9 0.0 copy-start.4
  3.9 0.7 copy-done.4
  4.6 0.0 copy-start.5
  4.6 0.7 copy-done.5
  5.3 67.4 %shard_map.139 = (bf16[32,1024]{1,0:T(8,128)(2,1)S(1)}, f32[1,1024]{1,0:T(1,128)S(1)}, f32[8,128]{1,0:T(8,128)S(1)}) custom-call(s32[512,1024]{1,0:T(8,128)} %spikes_h.1, s32[1,1024]{1,0:T(1,128)S(1)} %bitcast.8, bf16[1024,1024]{1,0:T(8,128)(2,1)} %readin_h.1, bf16[3,1024,512]{2,1,0:T(8,128)(2,1)} %bitcast.14, bf16[512,1024]{1,0:T(8,128)(2,1)S(1)} %copy-done, ...), custom_call_target="tpu_custom_call" | custom-call | flops 2147483648 | bytes 20971520 | tf_op jit(solution)/shard_map/pallas_call | solution.py:349
  72.7 0.5 slice.3
  73.2 0.6 copy.17
  73.8 0.6 copy.18
Async XLA Ops:
  0.6 1.2 %copy-start = (bf16[512,1024]{1,0:T(8,128)(2,1)S(1)}, bf16[512,1024]{1,0:T(8,128)(2,1)}, u32[]{:S(2)}) copy-start(bf16[512,1024]{1,0:T(8,128)(2,1)} %out_h.1) | copy-start | bytes 3145732
  1.9 0.7 copy-start.1
  2.5 0.7 copy-start.2
  3.2 0.7 copy-start.3
  3.9 0.7 copy-start.4
  4.6 0.7 copy-start.5

commit v2 on v1

--- a/solution.py
+++ b/solution.py
@@ -31,17 +31,17 @@
     n_size,
     t_size,
     spikes_h,
-    held_ref,
+    held_h,
     readin_h,
     qkv_h,
     out_h,
     up_h,
     down_h,
-    ng_ref,
-    mg_ref,
-    fg_ref,
+    ng_h,
+    mg_h,
+    fg_h,
     readout_h,
-    bias_ref,
+    bias_h,
     lat_out,
     bits_out,
     tot_out,
@@ -52,7 +52,13 @@
     up_v,
     down_v,
     readout_v,
+    held_ref,
+    ng_ref,
+    mg_ref,
+    fg_ref,
+    bias_ref,
     load_sems,
+    spike_sems,
     pp,
     core_s,
     core_r,
@@ -107,23 +113,47 @@
     loads = []
     for i, (src, dst) in enumerate(
         (
-            (spikes_h, spikes_v),
+            (held_h, held_ref),
             (readin_h, readin_v),
             (qkv_h, qkv_v),
             (out_h, out_v),
             (up_h, up_v),
             (down_h, down_v),
             (readout_h, readout_v),
+            (ng_h, ng_ref),
+            (mg_h, mg_ref),
+            (fg_h, fg_ref),
+            (bias_h, bias_ref),
         )
     ):
-        cp = pltpu.make_async_copy(src, dst, load_sems.at[i])
-        cp.start()
-        loads.append(cp)
-
-    peers = [core_peer()]
-    peers += [mid_peer(d) for d in range(1, mid_size)]
-    peers += [outer_peer(d) for d in range(1, OUTER)]
-    peers += [t_peer(d) for d in range(1, t_size)]
+        loads.append(pltpu.make_async_copy(src, dst, load_sems.at[i]))
+    order = [2, 1, 3, 0]
+    starts = {d: pl.multiple_of(rot(o, d, OUTER) * group, group) for d in order}
+    spike_loads = {}
+    for d in order:
+        at = pl.ds(starts[d], group)
+        spike_loads[d] = pltpu.make_async_copy(
+            spikes_h.at[at, :], spikes_v.at[at, :], spike_sems.at[d]
+        )
+    loads[0].start()
+    spike_loads[order[0]].start()
+    loads[1].start()
+    for d in order[1:]:
+        spike_loads[d].start()
+
+    plane = 2 * mid_size
+    line = OUTER * t_size
+
+    def plane_peer(d):
+        at = rot(m * 2 + c, d, plane)
+        return (o * plane + at, t)
+
+    def line_peer(d):
+        at = rot(o * t_size + t, d, line)
+        return (nid(lax.div(at, t_size), m, c), lax.rem(at, t_size))
+
+    peers = [plane_peer(d) for d in range(1, plane)]
+    peers += [line_peer(d) for d in range(1, line)]
     barrier = pltpu.get_barrier_semaphore()
     for peer in peers:
         pl.semaphore_signal(barrier, inc=1, device_id=peer, device_id_type=MESH)
@@ -143,12 +173,15 @@
         sent.append(cp)
         return cp
 
-    def sum_over_t(which, value):
-        tsum[which, t] = value.astype(BF)
-        cps = [
-            send(tsum.at[which, t], tsum.at[which, t], t_sems, (which, d), t_peer(d))
-            for d in range(1, t_size)
-        ]
+    def sum_over_t(which, pieces):
+        wide = width // len(pieces)
+        cps = []
+        for k, piece in enumerate(pieces):
+            cols = slice(k * wide, (k + 1) * wide)
+            tsum[which, t, :, cols] = piece().astype(BF)
+            for d in range(1, t_size):
+                part = tsum.at[which, t, :, cols]
+                cps.append(send(part, part, t_sems, (which, k, d), t_peer(d)))
         for cp in cps:
             cp.wait_recv()
         total = tsum[which, 0].astype(F32)
@@ -156,7 +189,7 @@
             total = total + tsum[which, i].astype(F32)
         return total
 
-    def gather(buf, sems):
+    def gather(buf, sems, use):
         cps = {}
 
         def push(do, dm, dc):
@@ -175,43 +208,48 @@
                 buf.at[block], buf.at[block], sems, ((do * mid_size + dm) * 2 + dc,), peer
             )
 
-        for d in range(1, OUTER):
-            push(d, 0, 0)
-        for d in range(1, mid_size):
-            push(0, d, 0)
-        push(0, 0, 1)
-        for d in range(1, mid_size):
-            cps[0, d, 0].wait_recv()
-            push(0, d, 1)
-        for do in (1, 3, 2):
-            cps[do, 0, 0].wait_recv()
+        def to_mid(do):
+            if do:
+                cps[do, 0, 0].wait_recv()
             for d in range(1, mid_size):
                 push(do, d, 0)
             push(do, 0, 1)
-        for do in (1, 3, 2):
+
+        def to_core(do):
             for d in range(1, mid_size):
                 cps[do, d, 0].wait_recv()
                 push(do, d, 1)
-        for do in range(OUTER):
+
+        def finish(do):
             for d in range(mid_size):
                 cps[do, d, 1].wait_recv()
-
-    loads[0].wait()
-    loads[1].wait()
-    held = held_ref[...]
-    order = [2, 1, 3, 0]
-    core_cps = {}
-    for k, d in enumerate(order):
-        at = pl.multiple_of(rot(o, d, OUTER) * group, group)
-        masked = (spikes_v[pl.ds(at, group), :] * held).astype(F32).astype(BF)
+            use(rot(o, OUTER - do, OUTER) * plane)
+
+        for d in (1, 3, 2):
+            push(d, 0, 0)
+        to_mid(0)
+        to_core(0)
+        last = 0
+        for do in (1, 3, 2):
+            to_mid(do)
+            finish(last)
+            to_core(do)
+            last = do
+        finish(last)
+
+    core_cps, mid_cps, outer_cps = {}, {}, {}
+
+    def read_in(d):
+        spike_loads[d].wait()
+        masked = (spikes_v[pl.ds(starts[d], group), :] * held_ref[...]).astype(F32).astype(BF)
         pp[d] = dot(masked, readin_v[...]).reshape(mid_size, 2, rows, width)
         for i in range(mid_size):
             core_s[d, i] = pp[d, i, 1 - c].astype(BF)
-        if k == 0:
+        if d == order[0]:
             pl.semaphore_wait(barrier, len(peers))
         core_cps[d] = send(core_s.at[d], core_r.at[d], core_sems, (d,), core_peer())
-    mid_cps = {}
-    for d in order:
+
+    def over_mid(d):
         core_cps[d].wait_recv()
         for dm in list(range(1, mid_size)) + [0]:
             mm = rot(m, dm, mid_size)
@@ -223,8 +261,8 @@
                 )
             else:
                 s1[d] = value
-    outer_cps = {}
-    for d in order:
+
+    def over_outer(d):
         value = s1[d]
         for dm in range(1, mid_size):
             mid_cps[d, dm].wait_recv()
@@ -232,31 +270,64 @@
         if d:
             out_s[d] = value.astype(BF)
             outer_cps[d] = send(out_s.at[d], out_r.at[d], outer_sems, (d,), outer_peer(d))
-    for d in (1, 3, 2):
+        return value
+
+    loads[0].wait()
+    loads[1].wait()
+    read_in(2)
+    for cp in loads[2:]:
+        cp.start()
+    read_in(1)
+    over_mid(2)
+    read_in(3)
+    over_mid(1)
+    over_outer(2)
+    read_in(0)
+    over_mid(3)
+    over_outer(1)
+    over_mid(0)
+    over_outer(3)
+    value = over_outer(0)
+    for d in (2, 1, 3):
         outer_cps[d].wait_recv()
         value = value + out_r[d].astype(F32)
-    stream = sum_over_t(0, value)
-
+    stream = sum_over_t(0, [lambda: value])
+
+    for cp in loads[7:]:
+        cp.wait()
     attn_in = normed(stream, ng_ref[...]).astype(BF)
     loads[2].wait()
     kv[n, :, :head_cols] = dot(attn_in, qkv_v[1]).astype(BF)
     kv[n, :, head_cols:] = dot(attn_in, qkv_v[2]).astype(BF)
     queries = dot(attn_in, qkv_v[0]).astype(BF)
-    gather(kv, kv_sems)
 
     scaling = 1.0 / math.sqrt(HEAD_DIM)
+    local_heads = head_cols // HEAD_DIM
+    numer = [jnp.zeros((rows, HEAD_DIM), F32)] * local_heads
+    denom = [jnp.zeros((rows, 1), F32)] * local_heads
+
+    def attend(base):
+        for h in range(local_heads):
+            cols = slice(h * HEAD_DIM, (h + 1) * HEAD_DIM)
+            vcols = slice(head_cols + h * HEAD_DIM, head_cols + (h + 1) * HEAD_DIM)
+            keys = kv[pl.ds(base, plane), :, cols].reshape(group, HEAD_DIM)
+            values = kv[pl.ds(base, plane), :, vcols].reshape(group, HEAD_DIM)
+            weights = jnp.exp(dot_nt(queries[:, cols], keys) * scaling)
+            denom[h] = denom[h] + jnp.sum(weights, -1, keepdims=True)
+            numer[h] = numer[h] + dot(weights.astype(BF), values)
+
+    gather(kv, kv_sems, attend)
     loads[3].wait()
-    heads = []
-    for h in range(head_cols // HEAD_DIM):
-        cols = slice(h * HEAD_DIM, (h + 1) * HEAD_DIM)
-        vcols = slice(head_cols + h * HEAD_DIM, head_cols + (h + 1) * HEAD_DIM)
-        keys = kv[:, :, cols].reshape(frames, HEAD_DIM)
-        values = kv[:, :, vcols].reshape(frames, HEAD_DIM)
-        weights = jnp.exp(dot_nt(queries[:, cols], keys) * scaling)
-        denominator = jnp.sum(weights, -1, keepdims=True)
-        heads.append((dot(weights.astype(BF), values) / denominator).astype(BF))
+    heads = [(a / b).astype(BF) for a, b in zip(numer, denom)]
     heads_out = heads[0] if len(heads) == 1 else jnp.concatenate(heads, -1)
-    mixed_state = stream + sum_over_t(1, dot(heads_out, out_v[...]))
+    half = width // 2
+    mixed_state = stream + sum_over_t(
+        1,
+        [
+            lambda: dot(heads_out, out_v[:, :half]),
+            lambda: dot(heads_out, out_v[:, half:]),
+        ],
+    )
 
     mlp_in = normed(mixed_state, mg_ref[...]).astype(BF)
     loads[4].wait()
@@ -265,26 +336,30 @@
         cols = slice(i * tile, (i + 1) * tile)
         hid[:, cols] = jax.nn.gelu(dot(mlp_in, up_v[:, cols])).astype(BF)
     loads[5].wait()
-    final_state = mixed_state + sum_over_t(2, dot(hid[...], down_v[...]))
+    final_state = mixed_state + sum_over_t(
+        2,
+        [
+            lambda: dot(hid[...], down_v[:, :half]),
+            lambda: dot(hid[...], down_v[:, half:]),
+        ],
+    )
     latents = normed(final_state, fg_ref[...]).astype(BF)
     lat_out[...] = latents
     lat[n] = latents
-    gather(lat, lat_sems)
-
     loads[6].wait()
-    blocks = 128 // rows
-
-    def readout_step(i, carry):
-        ll, counts = carry
-        at = pl.multiple_of(i * blocks * rows, blocks * rows)
-        piece = lat[pl.ds(i * blocks, blocks)].reshape(blocks * rows, width)
+    sums = [jnp.zeros((1, neurons), F32)] * 2
+
+    def read_out(base):
+        piece = lat[pl.ds(base, plane)].reshape(group, width)
+        at = pl.multiple_of(base * rows, group)
         log_rate = dot_nt(piece, readout_v[...]) + bias_ref[...]
-        observed = spikes_v[pl.ds(at, blocks * rows), :].astype(F32)
-        ll = ll + jnp.sum(observed * log_rate - jnp.exp(log_rate), 0, keepdims=True)
-        return ll, counts + jnp.sum(observed, 0, keepdims=True)
-
-    zero = jnp.zeros((1, neurons), F32)
-    model_ll, counts = lax.fori_loop(0, n_size // blocks, readout_step, (zero, zero))
+        observed = spikes_v[pl.ds(at, group), :].astype(F32)
+        sums[0] = sums[0] + jnp.sum(observed * log_rate - jnp.exp(log_rate), 0, keepdims=True)
+        sums[1] = sums[1] + jnp.sum(observed, 0, keepdims=True)
+
+    gather(lat, lat_sems, read_out)
+    model_ll, counts = sums
+    held = held_ref[...]
     heldout = (1 - held).astype(F32)
     null_ll = counts * jnp.log((counts + 1.0) / frames) - (counts + 1.0)
     gained = heldout * (model_ll - null_ll)
@@ -296,10 +371,8 @@
 
     base = 0
     for size, here, peer_of in (
-        (2, c, lambda d: core_peer()),
-        (mid_size, m, mid_peer),
-        (t_size, t, t_peer),
-        (OUTER, o, outer_peer),
+        (plane, m * 2 + c, plane_peer),
+        (line, o * t_size + t, line_peer),
     ):
         fin[base + here] = total
         cps = [
@@ -343,9 +416,9 @@
     qkv = qkv_weight.transpose(1, 0, 2)
     row = lambda v: v.reshape(1, -1)
     vmem = pl.BlockSpec(memory_space=pltpu.VMEM)
-    hbm = pl.BlockSpec(memory_space=pl.ANY)
+    hbm = pl.BlockSpec(memory_space=pltpu.HBM)
     dma = pltpu.SemaphoreType.DMA
-    n_fin = 2 + mid + t_size + OUTER
+    n_fin = 2 * mid + t_size * OUTER
     latents, bits, total = pl.pallas_call(
         functools.partial(kernel, n_size, t_size),
         out_shape=(
@@ -353,7 +426,7 @@
             jax.ShapeDtypeStruct((1, neurons), F32),
             jax.ShapeDtypeStruct((8, 128), F32),
         ),
-        in_specs=[hbm, vmem, hbm, hbm, hbm, hbm, hbm, vmem, vmem, vmem, hbm, vmem],
+        in_specs=[hbm] * 12,
         out_specs=(vmem, vmem, vmem),
         scratch_shapes=[
             pltpu.VMEM(spikes.shape, jnp.int32),
@@ -363,7 +436,13 @@
             pltpu.VMEM(up_weight.shape, BF),
             pltpu.VMEM(down_weight.shape, BF),
             pltpu.VMEM(readout_weight.shape, BF),
-            dma((7,)),
+            pltpu.VMEM((1, neurons), jnp.int32),
+            pltpu.VMEM((1, width), F32),
+            pltpu.VMEM((1, width), F32),
+            pltpu.VMEM((1, width), F32),
+            pltpu.VMEM((1, neurons), F32),
+            dma((11,)),
+            dma((OUTER,)),
             pltpu.VMEM((OUTER, mid, 2, rows, width), F32),
             pltpu.VMEM((OUTER, mid, rows, width), BF),
             pltpu.VMEM((OUTER, mid, rows, width), BF),
@@ -380,13 +459,13 @@
             dma((2, OUTER)),
             dma((2, OUTER * mid)),
             dma((2, OUTER)),
-            dma((2, 3, t_size)),
+            dma((2, 3, 2, t_size)),
             dma((2, n_size)),
             dma((2, n_size)),
             dma((2, n_fin)),
         ],
         compiler_params=pltpu.CompilerParams(
-            collective_id=0, has_side_effects=True, vmem_limit_bytes=52 * 1024 * 1024
+            collective_id=0, has_side_effects=True, vmem_limit_bytes=60 * 1024 * 1024
         ),
         cost_estimate=pl.CostEstimate(
             flops=4 * frames * neurons * width,

time: 74.7 us -> 76.2 us (1.020)
  Pallas kernels: 67.4 us -> 71.4 us
  local copies, waits for them, and re-layouts: 6.38 us -> 3.94 us
    pallas_call x1, Pallas kernels: 67.4 us -> 71.4 us  [on_device(): pl.pallas_call(functools.partial(kernel, n_size, t_size), out_shape=(jax....]
    unnamed x14 -> x2, local copies, waits for them, and re-layouts: 5.87 us -> 2.74 us
where the time goes in v2:
time: 76.2 us; the launch traced here: 76 us
  Pallas kernels  71.4 us (94%)
  local copies, waits for them, and re-layouts  3.94 us (5%)
    pallas_call x1, Pallas kernels, on_device(): pl.pallas_call(functools.partial(kernel, n_size, t_size), out_shape=(jax....  71.4 us
    unnamed x2, local copies, waits for them, and re-layouts  2.74 us

profile of v2, /device:TPU:0, one launch (start us, length us, event | category | flops | bytes accessed | tf_op | source)
XLA Modules:
  0.0 76.0 jit_solution(5976670999472459065)
XLA Ops:
  0.6 71.4 %shard_map.139 = (bf16[32,1024]{1,0:T(8,128)(2,1)}, f32[1,1024]{1,0:T(1,128)}, f32[8,128]{1,0:T(8,128)}) custom-call(s32[512,1024]{1,0:T(8,128)} %spikes_h.1, s32[1,1024]{1,0:T(1,128)} %bitcast.9, bf16[1024,1024]{1,0:T(8,128)(2,1)} %readin_h.1, bf16[3,1024,512]{2,1,0:T(8,128)(2,1)} %bitcast.8, bf16[512,1024]{1,0:T(8,128)(2,1)} %out_h.1, ...), custom_call_target="tpu_custom_call" | custom-call | flops 2147483648 | bytes 20971520 | tf_op jit(solution)/shard_map/pallas_call | solution.py:422
  72.1 1.2 %slice.3 = f32[1,1]{1,0:T(1,128)} slice(f32[8,128]{1,0:T(8,128)} %get-tuple-element.8), slice={[0:1], [0:1]} | slice | bytes 8 | tf_op jit(solution)/shard_map/slice | solution.py:489
  73.3 1.5 %copy.17 = bf16[32,1024]{1,0:T(8,128)(2,1)} copy(bf16[32,1024]{1,0:T(8,128)(2,1)} %get-tuple-element.12) | data formatting | bytes 131072
  74.7 1.3 %copy.18 = f32[1024]{0:T(1024)} copy(f32[1024]{0:T(1024)} %bitcast.14) | data formatting | bytes 8192

commit v3 on v2

--- a/solution.py
+++ b/solution.py
@@ -69,6 +69,9 @@
     out_r,
     tsum,
     kv,
+    pieces,
+    done_s,
+    done_r,
     lat,
     hid,
     fin,
@@ -225,17 +228,24 @@
                 cps[do, d, 1].wait_recv()
             use(rot(o, OUTER - do, OUTER) * plane)
 
-        for d in (1, 3, 2):
-            push(d, 0, 0)
+        push(1, 0, 0)
+        push(3, 0, 0)
         to_mid(0)
         to_core(0)
-        last = 0
-        for do in (1, 3, 2):
-            to_mid(do)
-            finish(last)
-            to_core(do)
-            last = do
-        finish(last)
+        for d in (1, 3):
+            cps[d, 0, 0].wait_send()
+            sent[:] = [cp for cp in sent if cp is not cps[d, 0, 0]]
+        push(2, 0, 0)
+        to_mid(1)
+        to_mid(3)
+        finish(0)
+        to_core(1)
+        to_core(3)
+        to_mid(2)
+        finish(1)
+        to_core(2)
+        finish(3)
+        finish(2)
 
     core_cps, mid_cps, outer_cps = {}, {}, {}
 
@@ -297,28 +307,75 @@
         cp.wait()
     attn_in = normed(stream, ng_ref[...]).astype(BF)
     loads[2].wait()
-    kv[n, :, :head_cols] = dot(attn_in, qkv_v[1]).astype(BF)
-    kv[n, :, head_cols:] = dot(attn_in, qkv_v[2]).astype(BF)
-    queries = dot(attn_in, qkv_v[0]).astype(BF)
-
+    projected = [dot(attn_in, qkv_v[i]).astype(BF) for i in range(3)]
+    loads[3].wait()
     scaling = 1.0 / math.sqrt(HEAD_DIM)
     local_heads = head_cols // HEAD_DIM
-    numer = [jnp.zeros((rows, HEAD_DIM), F32)] * local_heads
-    denom = [jnp.zeros((rows, 1), F32)] * local_heads
-
-    def attend(base):
-        for h in range(local_heads):
-            cols = slice(h * HEAD_DIM, (h + 1) * HEAD_DIM)
-            vcols = slice(head_cols + h * HEAD_DIM, head_cols + (h + 1) * HEAD_DIM)
-            keys = kv[pl.ds(base, plane), :, cols].reshape(group, HEAD_DIM)
-            values = kv[pl.ds(base, plane), :, vcols].reshape(group, HEAD_DIM)
-            weights = jnp.exp(dot_nt(queries[:, cols], keys) * scaling)
-            denom[h] = denom[h] + jnp.sum(weights, -1, keepdims=True)
-            numer[h] = numer[h] + dot(weights.astype(BF), values)
-
-    gather(kv, kv_sems, attend)
-    loads[3].wait()
-    heads = [(a / b).astype(BF) for a, b in zip(numer, denom)]
+    head_at = [slice(h * HEAD_DIM, (h + 1) * HEAD_DIM) for h in range(local_heads)]
+
+    def attend(query, keys, values, sums):
+        weights = jnp.exp(dot_nt(query, keys) * scaling)
+        return (
+            sums[0] + dot(weights.astype(BF), values),
+            sums[1] + jnp.sum(weights, -1, keepdims=True),
+        )
+
+    if local_heads == OUTER:
+        spot = m * 2 + c
+        for h in range(OUTER):
+            for i in range(3):
+                pieces[h, :, head_at[i]] = projected[i][:, head_at[h]]
+        turned = [
+            send(
+                pieces.at[rot(o, d, OUTER)], kv.at[spot, o], kv_sems, (d,), outer_peer(d)
+            )
+            for d in (2, 1, 3)
+        ]
+        kv[spot, o] = pieces[o]
+        for cp in turned:
+            cp.wait_recv()
+        spread = []
+        for d in range(1, plane):
+            part = kv.at[spot, :, :, HEAD_DIM : 3 * HEAD_DIM]
+            spread.append(send(part, part, kv_sems, (OUTER + d,), plane_peer(d)))
+        query = kv[spot, :, :, head_at[0]].reshape(OUTER * rows, HEAD_DIM)
+        sums = (jnp.zeros(query.shape, F32), jnp.zeros((OUTER * rows, 1), F32))
+        for d in range(plane):
+            if d:
+                spread[d - 1].wait_recv()
+            there = rot(spot, plane - d, plane)
+            keys = kv[there, :, :, head_at[1]].reshape(OUTER * rows, HEAD_DIM)
+            values = kv[there, :, :, head_at[2]].reshape(OUTER * rows, HEAD_DIM)
+            sums = attend(query, keys, values, sums)
+        done_s[...] = (sums[0] / sums[1]).astype(BF).reshape(OUTER, rows, HEAD_DIM)
+        back = [
+            send(
+                done_s.at[rot(o, d, OUTER)],
+                done_r.at[o],
+                kv_sems,
+                (OUTER + plane + d,),
+                outer_peer(d),
+            )
+            for d in (2, 1, 3)
+        ]
+        done_r[o] = done_s[o]
+        for cp in back:
+            cp.wait_recv()
+        heads = [done_r[h] for h in range(OUTER)]
+    else:
+        kv[n, :, :head_cols] = projected[1]
+        kv[n, :, head_cols:] = projected[2]
+        sums = [(jnp.zeros((rows, HEAD_DIM), F32), jnp.zeros((rows, 1), F32))] * local_heads
+
+        def attend_group(base):
+            for h in range(local_heads):
+                vcols = slice(head_cols + h * HEAD_DIM, head_cols + (h + 1) * HEAD_DIM)
+                keys = kv[pl.ds(base, plane), :, head_at[h]].reshape(group, HEAD_DIM)
+                values = kv[pl.ds(base, plane), :, vcols].reshape(group, HEAD_DIM)
+                sums[h] = attend(projected[0][:, head_at[h]], keys, values, sums[h])
+
+        gather(kv, kv_sems, attend_group)
+        heads = [(a / b).astype(BF) for a, b in sums]
     heads_out = heads[0] if len(heads) == 1 else jnp.concatenate(heads, -1)
     half = width // 2
     mixed_state = stream + sum_over_t(
@@ -418,6 +475,11 @@
     vmem = pl.BlockSpec(memory_space=pltpu.VMEM)
     hbm = pl.BlockSpec(memory_space=pltpu.HBM)
     dma = pltpu.SemaphoreType.DMA
+    by_head = head_cols == OUTER * HEAD_DIM
+    kv_shape = (
+        (2 * mid, OUTER, rows, 3 * HEAD_DIM) if by_head else (n_size, rows, 2 * head_cols)
+    )
+    n_kv = 2 * OUTER + 2 * mid if by_head else n_size
     n_fin = 2 * mid + t_size * OUTER
     latents, bits, total = pl.pallas_call(
         functools.partial(kernel, n_size, t_size),
@@ -452,7 +514,10 @@
             pltpu.VMEM((OUTER, rows, width), BF),
             pltpu.VMEM((OUTER, rows, width), BF),
             pltpu.VMEM((3, t_size, rows, width), BF),
-            pltpu.VMEM((n_size, rows, 2 * head_cols), BF),
+            pltpu.VMEM(kv_shape, BF),
+            pltpu.VMEM((OUTER, rows, 3 * HEAD_DIM), BF),
+            pltpu.VMEM((OUTER, rows, HEAD_DIM), BF),
+            pltpu.VMEM((OUTER, rows, HEAD_DIM), BF),
             pltpu.VMEM((n_size, rows, width), BF),
             pltpu.VMEM((rows, up_weight.shape[1]), BF),
             pltpu.VMEM((n_fin, 8, 128), F32),
@@ -460,12 +525,12 @@
             dma((2, OUTER * mid)),
             dma((2, OUTER)),
             dma((2, 3, 2, t_size)),
-            dma((2, n_size)),
+            dma((2, n_kv)),
             dma((2, n_size)),
             dma((2, n_fin)),
         ],
         compiler_params=pltpu.CompilerParams(
-            collective_id=0, has_side_effects=True, vmem_limit_bytes=60 * 1024 * 1024
+            collective_id=0, has_side_effects=True, vmem_limit_bytes=40 * 1024 * 1024
         ),
         cost_estimate=pl.CostEstimate(
             flops=4 * frames * neurons * width,

time: 76.2 us -> 79 us (1.037)
  local copies, waits for them, and re-layouts: 3.94 us -> 13 us
  Pallas kernels: 71.4 us -> 64.9 us
    unnamed x2 -> x22, local copies, waits for them, and re-layouts: 2.74 us -> 12.5 us
    pallas_call x1, Pallas kernels: 71.4 us -> 64.9 us  [on_device(): pl.pallas_call(functools.partial(kernel, n_size, t_size), out_shape=(jax....]
where the time goes in v3:
time: 79 us; the launch traced here: 78.6 us
  Pallas kernels  64.9 us (82%)
  local copies, waits for them, and re-layouts  13 us (16%)
    pallas_call x1, Pallas kernels, on_device(): pl.pallas_call(functools.partial(kernel, n_size, t_size), out_shape=(jax....  64.9 us
    unnamed x22, local copies, waits for them, and re-layouts  12.5 us

profile of v3, /device:TPU:0, one launch (start us, length us, event | category | flops | bytes accessed | tf_op | source)
XLA Modules:
  0.0 78.6 jit_solution(5863444716668579162)
XLA Ops:
  0.6 0.0 copy-start
  0.6 1.9 %copy-done = bf16[1024,3,512]{2,0,1:T(8,128)(2,1)S(1)} copy-done((bf16[1024,3,512]{2,0,1:T(8,128)(2,1)S(1)}, bf16[1024,3,512]{2,0,1:T(8,128)(2,1)}, u32[]{:S(2)}) %copy-start) | copy-done | bytes 3145752
  2.5 0.0 copy-start.1
  2.5 1.6 %copy-done.1 = s32[512,1024]{1,0:T(8,128)S(1)} copy-done((s32[512,1024]{1,0:T(8,128)S(1)}, s32[512,1024]{1,0:T(8,128)}, u32[]{:S(2)}) %copy-start.1) | copy-done | bytes 2097176
  4.1 0.0 copy-start.2
  4.1 1.6 %copy-done.2 = bf16[1024,1024]{1,0:T(8,128)(2,1)S(1)} copy-done((bf16[1024,1024]{1,0:T(8,128)(2,1)S(1)}, bf16[1024,1024]{1,0:T(8,128)(2,1)}, u32[]{:S(2)}) %copy-start.2) | copy-done | bytes 2097176
  5.7 0.0 copy-start.3
  5.7 1.6 %copy-done.3 = bf16[1024,1024]{1,0:T(8,128)(2,1)S(1)} copy-done((bf16[1024,1024]{1,0:T(8,128)(2,1)S(1)}, bf16[1024,1024]{1,0:T(8,128)(2,1)}, u32[]{:S(2)}) %copy-start.3) | copy-done | bytes 2097176
  7.3 0.0 copy-start.4
  7.3 1.2 %copy-done.4 = bf16[512,1024]{1,0:T(8,128)(2,1)S(1)} copy-done((bf16[512,1024]{1,0:T(8,128)(2,1)S(1)}, bf16[512,1024]{1,0:T(8,128)(2,1)}, u32[]{:S(2)}) %copy-start.4) | copy-done | bytes 1048600
  8.5 0.0 copy-start.5
  8.5 0.7 copy-done.5
  9.2 0.0 copy-start.6
  9.2 0.7 copy-done.6
  9.9 0.0 copy-start.7
  9.9 0.7 copy-done.7
  10.6 0.0 copy-start.8
  10.6 0.7 copy-done.8
  11.3 0.0 copy-start.9
  11.3 0.7 copy-done.9
  12.0 64.9 %shard_map.139 = (bf16[32,1024]{1,0:T(8,128)(2,1)S(1)}, f32[1,1024]{1,0:T(1,128)S(1)}, f32[8,128]{1,0:T(8,128)S(1)}) custom-call(s32[512,1024]{1,0:T(8,128)S(1)} %copy-done.1, s32[1,1024]{1,0:T(1,128)S(1)} %bitcast.9, bf16[1024,1024]{1,0:T(8,128)(2,1)S(1)} %copy-done.2, bf16[3,1024,512]{2,1,0:T(8,128)(2,1)S(1)} %bitcast.8, bf16[512,1024]{1,0:T(8,128)(2,1)S(1)} %copy-done.4, ...), custom_call_target="tpu_custom_call" | custom-call | flops 2147483648 | bytes 20971520 | tf_op jit(solution)/shard_map/pallas_call | solution.py:484
  76.8 0.5 slice.3
  77.3 0.6 copy.17
  78.0 0.6 copy.18
Async XLA Ops:
  0.6 1.9 %copy-start = (bf16[1024,3,512]{2,0,1:T(8,128)(2,1)S(1)}, bf16[1024,3,512]{2,0,1:T(8,128)(2,1)}, u32[]{:S(2)}) copy-start(bf16[1024,3,512]{2,0,1:T(8,128)(2,1)} %param.15) | copy-start | bytes 9437188
  2.5 1.6 %copy-start.1 = (s32[512,1024]{1,0:T(8,128)S(1)}, s32[512,1024]{1,0:T(8,128)}, u32[]{:S(2)}) copy-start(s32[512,1024]{1,0:T(8,128)} %spikes_h.1) | copy-start | bytes 6291460
  4.1 1.6 %copy-start.2 = (bf16[1024,1024]{1,0:T(8,128)(2,1)S(1)}, bf16[1024,1024]{1,0:T(8,128)(2,1)}, u32[]{:S(2)}) copy-start(bf16[1024,1024]{1,0:T(8,128)(2,1)} %readin_h.1) | copy-start | bytes 6291460
  5.7 1.6 %copy-start.3 = (bf16[1024,1024]{1,0:T(8,128)(2,1)S(1)}, bf16[1024,1024]{1,0:T(8,128)(2,1)}, u32[]{:S(2)}) copy-start(bf16[1024,1024]{1,0:T(8,128)(2,1)} %readout_h.1) | copy-start | bytes 6291460
  7.3 1.2 %copy-start.4 = (bf16[512,1024]{1,0:T(8,128)(2,1)S(1)}, bf16[512,1024]{1,0:T(8,128)(2,1)}, u32[]{:S(2)}) copy-start(bf16[512,1024]{1,0:T(8,128)(2,1)} %out_h.1) | copy-start | bytes 3145732
  8.5 0.7 copy-start.5
  9.2 0.7 copy-start.6
  9.9 0.7 copy-start.7
  10.6 0.7 copy-start.8
  11.3 0.7 copy-start.9

commit v4 on v3

--- a/solution.py
+++ b/solution.py
@@ -117,7 +117,6 @@
     for i, (src, dst) in enumerate(
         (
             (held_h, held_ref),
-            (readin_h, readin_v),
             (qkv_h, qkv_v),
             (out_h, out_v),
             (up_h, up_v),
@@ -138,9 +137,17 @@
         spike_loads[d] = pltpu.make_async_copy(
             spikes_h.at[at, :], spikes_v.at[at, :], spike_sems.at[d]
         )
+    quarter = readin_v.shape[0] // 4
+    readin_loads = []
+    for i in range(4):
+        at = pl.ds(i * quarter, quarter)
+        readin_loads.append(
+            pltpu.make_async_copy(readin_h.at[at, :], readin_v.at[at, :], spike_sems.at[OUTER + i])
+        )
     loads[0].start()
     spike_loads[order[0]].start()
-    loads[1].start()
+    for cp in readin_loads:
+        cp.start()
     for d in order[1:]:
         spike_loads[d].start()
 
@@ -283,9 +290,10 @@
         return value
 
     loads[0].wait()
-    loads[1].wait()
+    for cp in readin_loads:
+        cp.wait()
     read_in(2)
-    for cp in loads[2:]:
+    for cp in loads[1:]:
         cp.start()
     read_in(1)
     over_mid(2)
@@ -303,12 +311,12 @@
         value = value + out_r[d].astype(F32)
     stream = sum_over_t(0, [lambda: value])
 
-    for cp in loads[7:]:
+    for cp in loads[6:]:
         cp.wait()
     attn_in = normed(stream, ng_ref[...]).astype(BF)
+    loads[1].wait()
+    projected = [dot(attn_in, qkv_v[i]).astype(BF) for i in range(3)]
     loads[2].wait()
-    projected = [dot(attn_in, qkv_v[i]).astype(BF) for i in range(3)]
-    loads[3].wait()
     scaling = 1.0 / math.sqrt(HEAD_DIM)
     local_heads = head_cols // HEAD_DIM
     head_at = [slice(h * HEAD_DIM, (h + 1) * HEAD_DIM) for h in range(local_heads)]
@@ -387,12 +395,12 @@
     )
 
     mlp_in = normed(mixed_state, mg_ref[...]).astype(BF)
-    loads[4].wait()
+    loads[3].wait()
     tile = min(512, up_v.shape[1])
     for i in range(up_v.shape[1] // tile):
         cols = slice(i * tile, (i + 1) * tile)
         hid[:, cols] = jax.nn.gelu(dot(mlp_in, up_v[:, cols])).astype(BF)
-    loads[5].wait()
+    loads[4].wait()
     final_state = mixed_state + sum_over_t(
         2,
         [
@@ -403,7 +411,7 @@
     latents = normed(final_state, fg_ref[...]).astype(BF)
     lat_out[...] = latents
     lat[n] = latents
-    loads[6].wait()
+    loads[5].wait()
     sums = [jnp.zeros((1, neurons), F32)] * 2
 
     def read_out(base):
@@ -436,6 +444,9 @@
             send(fin.at[base + here], fin.at[base + here], fin_sems, (base + d,), peer_of(d))
             for d in range(1, size)
         ]
+        if base:
+            for cp in sent:
+                cp.wait_send()
         for cp in cps:
             cp.wait_recv()
         total = fin[base]
@@ -445,8 +456,12 @@
     score = jnp.sum(jnp.where(lane == 0, total, 0.0), -1, keepdims=True)
     spike_sum = jnp.sum(jnp.where(lane == 1, total, 0.0), -1, keepdims=True)
     tot_out[...] = jnp.broadcast_to(score / (math.log(2.0) * (1.0 + spike_sum)), (8, 128))
-    for cp in sent:
-        cp.wait_send()
+
+
+def hand_over(lat_ref, bits_ref, tot_ref, lat_out, bits_out, tot_out):
+    lat_out[...] = lat_ref[...]
+    bits_out[...] = bits_ref[...]
+    tot_out[...] = tot_ref[0:1, 0:1]
 
 
 def on_device(
@@ -503,8 +518,8 @@
             pltpu.VMEM((1, width), F32),
             pltpu.VMEM((1, width), F32),
             pltpu.VMEM((1, neurons), F32),
-            dma((11,)),
-            dma((OUTER,)),
+            dma((10,)),
+            dma((OUTER + 4,)),
             pltpu.VMEM((OUTER, mid, 2, rows, width), F32),
             pltpu.VMEM((OUTER, mid, rows, width), BF),
             pltpu.VMEM((OUTER, mid, rows, width), BF),
@@ -530,7 +545,7 @@
             dma((2, n_fin)),
         ],
         compiler_params=pltpu.CompilerParams(
-            collective_id=0, has_side_effects=True, vmem_limit_bytes=40 * 1024 * 1024
+            collective_id=0, has_side_effects=True, vmem_limit_bytes=60 * 1024 * 1024
         ),
         cost_estimate=pl.CostEstimate(
             flops=4 * frames * neurons * width,
@@ -551,7 +566,18 @@
         readout_weight,
         row(readout_bias),
     )
-    return latents, bits.reshape(neurons), total[0, 0]
+    latents, bits, total = pl.pallas_call(
+        hand_over,
+        out_shape=(
+            jax.ShapeDtypeStruct((rows, width), BF),
+            jax.ShapeDtypeStruct((1, neurons), F32),
+            jax.ShapeDtypeStruct((1, 1), F32),
+        ),
+        in_specs=[vmem] * 3,
+        out_specs=(vmem, vmem, vmem),
+        compiler_params=pltpu.CompilerParams(vmem_limit_bytes=60 * 1024 * 1024),
+    )(latents, bits, total)
+    return latents, bits.reshape(neurons), total.reshape(())
 
 
 def solution(mesh):

time: 79 us -> 67.5 us (0.85)
  local copies, waits for them, and re-layouts: 13 us -> 0 us
  Pallas kernels: 64.9 us -> 66.7 us
    unnamed x22 -> x0, local copies, waits for them, and re-layouts: 12.5 us -> none
    pallas_call x0 -> x1, Pallas kernels: none -> 1.48 us  [on_device(): pl.pallas_call(hand_over, out_shape=(jax.ShapeDtypeStruct((rows, width),...]
where the time goes in v4:
time: 67.5 us; the launch traced here: 67.4 us
  Pallas kernels  66.7 us (99%)
    pallas_call x1, Pallas kernels, on_device(): pl.pallas_call(functools.partial(kernel, n_size, t_size), out_shape=(jax....  65.2 us
    pallas_call x1, Pallas kernels, on_device(): pl.pallas_call(hand_over, out_shape=(jax.ShapeDtypeStruct((rows, width),...  1.48 us

profile of v4, /device:TPU:0, one launch (start us, length us, event | category | flops | bytes accessed | tf_op | source)
XLA Modules:
  0.0 67.4 jit_solution(15516313555298497685)
XLA Ops:
  0.6 65.2 %shard_map.139 = (bf16[32,1024]{1,0:T(8,128)(2,1)}, f32[1,1024]{1,0:T(1,128)}, f32[8,128]{1,0:T(8,128)}) custom-call(s32[512,1024]{1,0:T(8,128)} %spikes_h.1, s32[1,1024]{1,0:T(1,128)} %bitcast.9, bf16[1024,1024]{1,0:T(8,128)(2,1)} %readin_h.1, bf16[3,1024,512]{2,1,0:T(8,128)(2,1)} %bitcast.8, bf16[512,1024]{1,0:T(8,128)(2,1)} %out_h.1, ...), custom_call_target="tpu_custom_call" | custom-call | flops 2147483648 | bytes 20971520 | tf_op jit(solution)/shard_map/pallas_call | solution.py:499
  65.9 1.5 %shard_map.140 = (bf16[32,1024]{1,0:T(8,128)(2,1)}, f32[1,1024]{1,0:T(1,128)}, f32[1,1]{1,0:T(1,128)}) custom-call(bf16[32,1024]{1,0:T(8,128)(2,1)} %get-tuple-element.9.lat_ref, f32[1,1024]{1,0:T(1,128)} %get-tuple-element.10.bits_ref, f32[8,128]{1,0:T(8,128)} %get-tuple-element.11.tot_ref), custom_call_target="tpu_custom_call" | custom-call | tf_op jit(solution)/shard_map/pallas_call | solution.py:569

commit v5 on v4

--- a/solution.py
+++ b/solution.py
@@ -299,11 +299,11 @@
     over_mid(2)
     read_in(3)
     over_mid(1)
-    over_outer(2)
     read_in(0)
     over_mid(3)
+    over_outer(2)
+    over_mid(0)
     over_outer(1)
-    over_mid(0)
     over_outer(3)
     value = over_outer(0)
     for d in (2, 1, 3):
@@ -315,8 +315,10 @@
         cp.wait()
     attn_in = normed(stream, ng_ref[...]).astype(BF)
     loads[1].wait()
-    projected = [dot(attn_in, qkv_v[i]).astype(BF) for i in range(3)]
-    loads[2].wait()
+
+    def project(i):
+        return dot(attn_in, qkv_v[i]).astype(BF)
+
     scaling = 1.0 / math.sqrt(HEAD_DIM)
     local_heads = head_cols // HEAD_DIM
     head_at = [slice(h * HEAD_DIM, (h + 1) * HEAD_DIM) for h in range(local_heads)]
@@ -330,27 +332,53 @@
 
     if local_heads == OUTER:
         spot = m * 2 + c
+        key_value = slice(HEAD_DIM, 3 * HEAD_DIM)
+
+        def turn(cols, base):
+            return {
+                d: send(
+                    pieces.at[rot(o, d, OUTER), :, cols],
+                    kv.at[spot, o, :, cols],
+                    kv_sems,
+                    (base + d,),
+                    outer_peer(d),
+                )
+                for d in (2, 1, 3)
+            }
+
+        spread = {}
+
+        def into_plane(do):
+            there = rot(o, OUTER - do, OUTER)
+            for d in range(1, plane):
+                part = kv.at[spot, there, :, key_value]
+                spread[do, d] = send(
+                    part, part, kv_sems, (2 * OUTER + do * plane + d,), plane_peer(d)
+                )
+
+        for i in (1, 2):
+            piece = project(i)
+            for h in range(OUTER):
+                pieces[h, :, head_at[i]] = piece[:, head_at[h]]
+        turned = turn(key_value, 0)
+        kv[spot, o, :, key_value] = pieces[o, :, key_value]
+        into_plane(0)
+        piece = project(0)
         for h in range(OUTER):
-            for i in range(3):
-                pieces[h, :, head_at[i]] = projected[i][:, head_at[h]]
-        turned = [
-            send(
-                pieces.at[rot(o, d, OUTER)], kv.at[spot, o], kv_sems, (d,), outer_peer(d)
-            )
-            for d in (2, 1, 3)
-        ]
-        kv[spot, o] = pieces[o]
-        for cp in turned:
-            cp.wait_recv()
-        spread = []
-        for d in range(1, plane):
-            part = kv.at[spot, :, :, HEAD_DIM : 3 * HEAD_DIM]
-            spread.append(send(part, part, kv_sems, (OUTER + d,), plane_peer(d)))
+            pieces[h, :, head_at[0]] = piece[:, head_at[h]]
+        turned_query = turn(head_at[0], OUTER)
+        kv[spot, o, :, head_at[0]] = pieces[o, :, head_at[0]]
+        for d in (1, 3, 2):
+            turned[d].wait_recv()
+            into_plane(d)
+        for d in (1, 3, 2):
+            turned_query[d].wait_recv()
         query = kv[spot, :, :, head_at[0]].reshape(OUTER * rows, HEAD_DIM)
         sums = (jnp.zeros(query.shape, F32), jnp.zeros((OUTER * rows, 1), F32))
         for d in range(plane):
             if d:
-                spread[d - 1].wait_recv()
+                for do in range(OUTER):
+                    spread[do, d].wait_recv()
             there = rot(spot, plane - d, plane)
             keys = kv[there, :, :, head_at[1]].reshape(OUTER * rows, HEAD_DIM)
             values = kv[there, :, :, head_at[2]].reshape(OUTER * rows, HEAD_DIM)
@@ -361,7 +389,7 @@
                 done_s.at[rot(o, d, OUTER)],
                 done_r.at[o],
                 kv_sems,
-                (OUTER + plane + d,),
+                ((2 + plane) * OUTER + d,),
                 outer_peer(d),
             )
             for d in (2, 1, 3)
@@ -371,6 +399,7 @@
             cp.wait_recv()
         heads = [done_r[h] for h in range(OUTER)]
     else:
+        projected = [project(i) for i in range(3)]
         kv[n, :, :head_cols] = projected[1]
         kv[n, :, head_cols:] = projected[2]
         sums = [(jnp.zeros((rows, HEAD_DIM), F32), jnp.zeros((rows, 1), F32))] * local_heads
@@ -384,6 +413,7 @@
 
         gather(kv, kv_sems, attend_group)
         heads = [(a / b).astype(BF) for a, b in sums]
+    loads[2].wait()
     heads_out = heads[0] if len(heads) == 1 else jnp.concatenate(heads, -1)
     half = width // 2
     mixed_state = stream + sum_over_t(
@@ -494,7 +524,7 @@
     kv_shape = (
         (2 * mid, OUTER, rows, 3 * HEAD_DIM) if by_head else (n_size, rows, 2 * head_cols)
     )
-    n_kv = 2 * OUTER + 2 * mid if by_head else n_size
+    n_kv = (3 + 2 * mid) * OUTER if by_head else n_size
     n_fin = 2 * mid + t_size * OUTER
     latents, bits, total = pl.pallas_call(
         functools.partial(kernel, n_size, t_size),

time: 67.5 us -> 66.9 us (level)
  no operation moved by 1% of the time
where the time goes in v5:
time: 66.9 us; the launch traced here: 66.8 us
  Pallas kernels  66.1 us (99%)
    pallas_call x1, Pallas kernels, on_device(): pl.pallas_call(functools.partial(kernel, n_size, t_size), out_shape=(jax....  64.6 us
    pallas_call x1, Pallas kernels, on_device(): pl.pallas_call(hand_over, out_shape=(jax.ShapeDtypeStruct((rows, width),...  1.48 us

profile of v5, /device:TPU:0, one launch (start us, length us, event | category | flops | bytes accessed | tf_op | source)
XLA Modules:
  0.0 66.8 jit_solution(5732649474984226999)
XLA Ops:
  0.6 64.6 %shard_map.139 = (bf16[32,1024]{1,0:T(8,128)(2,1)}, f32[1,1024]{1,0:T(1,128)}, f32[8,128]{1,0:T(8,128)}) custom-call(s32[512,1024]{1,0:T(8,128)} %spikes_h.1, s32[1,1024]{1,0:T(1,128)} %bitcast.9, bf16[1024,1024]{1,0:T(8,128)(2,1)} %readin_h.1, bf16[3,1024,512]{2,1,0:T(8,128)(2,1)} %bitcast.8, bf16[512,1024]{1,0:T(8,128)(2,1)} %out_h.1, ...), custom_call_target="tpu_custom_call" | custom-call | flops 2147483648 | bytes 20971520 | tf_op jit(solution)/shard_map/pallas_call | solution.py:529
  65.3 1.5 %shard_map.140 = (bf16[32,1024]{1,0:T(8,128)(2,1)}, f32[1,1024]{1,0:T(1,128)}, f32[1,1]{1,0:T(1,128)}) custom-call(bf16[32,1024]{1,0:T(8,128)(2,1)} %get-tuple-element.9.lat_ref, f32[1,1024]{1,0:T(1,128)} %get-tuple-element.10.bits_ref, f32[8,128]{1,0:T(8,128)} %get-tuple-element.11.tot_ref), custom_call_target="tpu_custom_call" | custom-call | tf_op jit(solution)/shard_map/pallas_call | solution.py:599

commit v6 on v5

--- a/solution.py
+++ b/solution.py
@@ -10,6 +10,7 @@
 
 HEAD_DIM = 128
 OUTER = 4
+TILE = 256
 MESH = pl.DeviceIdType.MESH
 BF = jnp.bfloat16
 F32 = jnp.float32
@@ -75,6 +76,8 @@
     lat,
     hid,
     fin,
+    mask_v,
+    acc,
     core_sems,
     mid_sems,
     outer_sems,
@@ -258,8 +261,18 @@
 
     def read_in(d):
         spike_loads[d].wait()
-        masked = (spikes_v[pl.ds(starts[d], group), :] * held_ref[...]).astype(F32).astype(BF)
-        pp[d] = dot(masked, readin_v[...]).reshape(mid_size, 2, rows, width)
+        mask_v[...] = (
+            (spikes_v[pl.ds(starts[d], group), :] * held_ref[...]).astype(F32).astype(BF)
+        )
+
+        def columns(j, carry):
+            cols = pl.ds(pl.multiple_of(j * TILE, TILE), TILE)
+            pp[d, :, :, :, cols] = dot(mask_v[...], readin_v[:, cols]).reshape(
+                mid_size, 2, rows, TILE
+            )
+            return carry
+
+        lax.fori_loop(0, width // TILE, columns, 0)
         for i in range(mid_size):
             core_s[d, i] = pp[d, i, 1 - c].astype(BF)
         if d == order[0]:
@@ -426,10 +439,13 @@
 
     mlp_in = normed(mixed_state, mg_ref[...]).astype(BF)
     loads[3].wait()
-    tile = min(512, up_v.shape[1])
-    for i in range(up_v.shape[1] // tile):
-        cols = slice(i * tile, (i + 1) * tile)
+
+    def up_columns(j, carry):
+        cols = pl.ds(pl.multiple_of(j * TILE, TILE), TILE)
         hid[:, cols] = jax.nn.gelu(dot(mlp_in, up_v[:, cols])).astype(BF)
+        return carry
+
+    lax.fori_loop(0, up_v.shape[1] // TILE, up_columns, 0)
     loads[4].wait()
     final_state = mixed_state + sum_over_t(
         2,
@@ -442,18 +458,24 @@
     lat_out[...] = latents
     lat[n] = latents
     loads[5].wait()
-    sums = [jnp.zeros((1, neurons), F32)] * 2
+    acc[...] = jnp.zeros(acc.shape, F32)
 
     def read_out(base):
-        piece = lat[pl.ds(base, plane)].reshape(group, width)
         at = pl.multiple_of(base * rows, group)
-        log_rate = dot_nt(piece, readout_v[...]) + bias_ref[...]
-        observed = spikes_v[pl.ds(at, group), :].astype(F32)
-        sums[0] = sums[0] + jnp.sum(observed * log_rate - jnp.exp(log_rate), 0, keepdims=True)
-        sums[1] = sums[1] + jnp.sum(observed, 0, keepdims=True)
+
+        def columns(j, carry):
+            cols = pl.ds(pl.multiple_of(j * TILE, TILE), TILE)
+            piece = lat[pl.ds(base, plane)].reshape(group, width)
+            log_rate = dot_nt(piece, readout_v[cols, :]) + bias_ref[:, cols]
+            observed = spikes_v[pl.ds(at, group), cols].astype(F32)
+            acc[0, :, cols] += jnp.sum(observed * log_rate - jnp.exp(log_rate), 0, keepdims=True)
+            acc[1, :, cols] += jnp.sum(observed, 0, keepdims=True)
+            return carry
+
+        lax.fori_loop(0, neurons // TILE, columns, 0)
 
     gather(lat, lat_sems, read_out)
-    model_ll, counts = sums
+    model_ll, counts = acc[0], acc[1]
     held = held_ref[...]
     heldout = (1 - held).astype(F32)
     null_ll = counts * jnp.log((counts + 1.0) / frames) - (counts + 1.0)
@@ -566,6 +588,8 @@
             pltpu.VMEM((n_size, rows, width), BF),
             pltpu.VMEM((rows, up_weight.shape[1]), BF),
             pltpu.VMEM((n_fin, 8, 128), F32),
+            pltpu.VMEM((2 * mid * rows, neurons), BF),
+            pltpu.VMEM((2, 1, neurons), F32),
             dma((2, OUTER)),
             dma((2, OUTER * mid)),
             dma((2, OUTER)),

time: 66.9 us -> 67.8 us (1.013)
  Pallas kernels: 66.1 us -> 67 us
    pallas_call x1, Pallas kernels: 64.6 us -> 65.5 us  [on_device(): pl.pallas_call(functools.partial(kernel, n_size, t_size), out_shape=(jax....]
where the time goes in v6:
time: 67.8 us; the launch traced here: 67.7 us
  Pallas kernels  67 us (99%)
    pallas_call x1, Pallas kernels, on_device(): pl.pallas_call(functools.partial(kernel, n_size, t_size), out_shape=(jax....  65.5 us
    pallas_call x1, Pallas kernels, on_device(): pl.pallas_call(hand_over, out_shape=(jax.ShapeDtypeStruct((rows, width),...  1.48 us

profile of v6, /device:TPU:0, one launch (start us, length us, event | category | flops | bytes accessed | tf_op | source)
XLA Modules:
  0.0 67.7 jit_solution(12275052457722869123)
XLA Ops:
  0.6 65.5 %shard_map.139 = (bf16[32,1024]{1,0:T(8,128)(2,1)}, f32[1,1024]{1,0:T(1,128)}, f32[8,128]{1,0:T(8,128)}) custom-call(s32[512,1024]{1,0:T(8,128)} %spikes_h.1, s32[1,1024]{1,0:T(1,128)} %bitcast.9, bf16[1024,1024]{1,0:T(8,128)(2,1)} %readin_h.1, bf16[3,1024,512]{2,1,0:T(8,128)(2,1)} %bitcast.8, bf16[512,1024]{1,0:T(8,128)(2,1)} %out_h.1, ...), custom_call_target="tpu_custom_call" | custom-call | flops 2147483648 | bytes 20971520 | tf_op jit(solution)/shard_map/pallas_call | solution.py:551
  66.2 1.5 %shard_map.140 = (bf16[32,1024]{1,0:T(8,128)(2,1)}, f32[1,1024]{1,0:T(1,128)}, f32[1,1]{1,0:T(1,128)}) custom-call(bf16[32,1024]{1,0:T(8,128)(2,1)} %get-tuple-element.9.lat_ref, f32[1,1024]{1,0:T(1,128)} %get-tuple-element.10.bits_ref, f32[8,128]{1,0:T(8,128)} %get-tuple-element.11.tot_ref), custom_call_target="tpu_custom_call" | custom-call | tf_op jit(solution)/shard_map/pallas_call | solution.py:623
